TPU v7x, 32 devices: a whole 2x2x4 slice. The times are simulated.
32 devices in a mesh: leaf: 8 (over z, x), grp: 4 (over y, core).
Axes of the slice: x: 2, y: 2, z: 4, core: 2. Of those that a mesh axis runs over, the one named last changes fastest.
Arguments:
- vectors: float32 [16, 262144], P(None, ('leaf', 'grp')), may hold values from -6 to 6
- coords: float32 [2, 262144], P(None, ('leaf', 'grp')), may hold values from 0 to 1, as said below
- perm: int32 [262144], P(('leaf', 'grp')), may hold values from 0 to 8191, as said below
- bases: float32 [512, 64, 512], P(('leaf', 'grp')), may hold values from -0.25 to 0.25
- leaf_maps: float32 [512, 64, 64], P(('leaf', 'grp')), may hold values from -0.1875 to 0.1875
- node_maps: float32 [32, 64, 64], P(('leaf', 'grp')), may hold values from -0.375 to 0.375
- leaf_skel: float32 [512, 2, 64], P(('leaf', 'grp')), may hold values from 0 to 1
- node_skel: float32 [32, 2, 64], P(('leaf', 'grp')), may hold values from 0 to 1
- sub_skel: float32 [8, 2, 64], P('leaf'), may hold values from 0 to 1
- leaf_src: int32 [512, 16], P(('leaf', 'grp')), may hold values from 0 to 63
- leaf_count: int32 [512], P(('leaf', 'grp')), may hold values from 1 to 16
- node_src: int32 [32, 8], P(('leaf', 'grp')), may hold values from 0 to 11, as said below
- node_count: int32 [32], P(('leaf', 'grp')), may hold values from 1 to 8
Outputs:
- product: float32 [16, 262144], P(None, ('leaf', 'grp'))
Inputs may be any that keep to these rules, and one draw needn't show every extreme that they name: `perm`: each aligned block of 8192 entries holds every number of 0 to 8191 once. `coords`: rows 3k, 3k + 1 and 3k + 2 share one site's coordinates. `node_src`: entries index the device nodes of subtrees s - 1, s, s + 1 in order (s the node's own subtree), only subtrees that exist.
All inputs are finite; a program needn't handle non-finite values.
Results may differ from a plain program's by a relative error of at most 0.0003.
Values sent between devices are 32-bit elements; how exact they have to be, the bound alone decides.
No kernel may reach another device: no remote copies, remote signals or barrier semaphores. Data moves between devices by JAX's collectives and lax.ppermute only.
A program may use at most 64 MiB of HBM per device.

v0:
```python
import functools
import math

import jax
import jax.numpy as jnp
import numpy as np
from jax import lax
from jax.experimental import pallas as pl
from jax.experimental.pallas import tpu as pltpu
from jax.sharding import PartitionSpec as P

F32 = jnp.float32
BF16 = jnp.bfloat16
WIDE = 128
SHIFT = 7
LOG2E = math.log2(math.e)
TINY = 1e-37
PACK_ROWS = 24
PART = 32
AT_ONCE = 8


def make_tables(norm):
    smooth = [0, 2, 4]
    sigmas = [1.0, 0.8, 1.2]
    rho = [[1.0, 0.5, 0.3], [0.5, 1.0, 0.4], [0.3, 0.4, 1.0]]
    scale = np.zeros((3, 3))
    poly = np.zeros((5, 3, 3))
    for first in range(3):
        for second in range(3):
            order = (smooth[first] + smooth[second]) // 2
            scale[first, second] = -(2.0 * order + 1.0) * (LOG2E / 0.3) ** 2
            amp = sigmas[first] * sigmas[second] * rho[first][second] * norm
            for power in range(order + 1):
                kterm = order - power
                coeff = math.factorial(order) / math.factorial(2 * order)
                coeff = (
                    coeff
                    * math.factorial(order + kterm)
                    / (math.factorial(kterm) * math.factorial(order - kterm))
                )
                poly[power, first, second] = amp * coeff * 2.0**power * (-1.0 / LOG2E) ** power
    return scale, poly


def dot(one, two, turned=False):
    dims = (((1,), (1 if turned else 0,)), ((), ()))
    return lax.dot_general(one, two, dims, preferred_element_type=F32)


def parts(value):
    high = value.astype(BF16)
    return high, (value - high.astype(F32)).astype(BF16)


def product(one, two, turned=False):
    rows = one.shape[0]
    one_hi, one_lo = parts(one)
    two_hi, two_lo = parts(two)
    both = dot(jnp.concatenate([one_hi, one_lo], axis=0), two_hi, turned)
    return both[:rows] + both[rows:] + dot(one_hi, two_lo, turned)


def count_rows(rows):
    rows[...] = lax.broadcasted_iota(jnp.int32, rows.shape, 0).astype(jnp.int16)


def one_hot(rows, low):
    count = low.shape[1]
    low = jnp.broadcast_to(low, (16, count)).astype(jnp.int16)[None]
    same = rows[:, :count].reshape(WIDE // 16, 16, count) == low
    return jnp.where(same, jnp.bfloat16(1), jnp.bfloat16(0)).reshape(WIDE, count)


def fill(source, value, at, nvec):
    high, low = parts(value)
    source[pl.ds(at, nvec), :WIDE] = high
    source[pl.ds(at, nvec), WIDE:] = low


def pick(rows, source, index, nvec):
    count = index.shape[1]
    hot = one_hot(rows, index & (WIDE - 1))
    hot = jnp.concatenate([hot, hot], axis=0)
    chunk = jnp.broadcast_to(index >> SHIFT, (8, count))[None]
    out = jnp.zeros((nvec // 8, 8, count), F32)
    chunks = source.shape[0] // nvec
    found = dot(source[...], hot).reshape(chunks, nvec // 8, 8, count)
    for each in range(chunks):
        out = jnp.where(chunk == each, found[each], out)
    return out.reshape(nvec, count)


def leaf_index(perm, leaf, block):
    rows = block // 128
    return jnp.concatenate([perm[pl.ds(leaf * rows + each, 1), :] for each in range(rows)], axis=1)


def fetch(pairs, sems):
    copies = [pltpu.make_async_copy(src, dst, sems.at[each]) for each, (src, dst) in enumerate(pairs)]
    for copy in copies:
        copy.start()
    return copies


def up_kernel(*refs):
    given, (tree_out, leaf_pack, tree_pack) = refs[:8], refs[8:11]
    held = refs[11:19]
    tree_vec, source, rows, sems = refs[19:]
    count_rows(rows)
    copies = fetch(list(zip(given, held)), sems)
    vec, perm, bases, leaf_maps, node_maps, leaf_skel, node_skel, sub_skel = held
    leaves, nvec, block = tree_vec.shape
    rank = bases.shape[1]
    copies[0].wait()
    for each in range(vec.shape[1] // WIDE):
        fill(source, vec[:, each * WIDE : (each + 1) * WIDE], each * nvec, nvec)
    copies[1].wait()

    def gather(leaf, carry):
        tree_vec[leaf] = pick(rows, source, leaf_index(perm, leaf, block), nvec)
        return carry

    lax.fori_loop(0, leaves, gather, 0, unroll=8)
    leave = pltpu.make_async_copy(tree_vec, tree_out, sems.at[len(copies)])
    leave.start()
    for copy in copies[2:]:
        copy.wait()
    up_node = jnp.zeros((nvec, rank), F32)
    blank = jnp.zeros((PACK_ROWS - nvec - 2, 2 * rank), F32)
    for leaf in range(0, leaves, 2):
        up = [product(tree_vec[leaf + each], bases[leaf + each], True) for each in range(2)]
        leaf_pack[leaf // 2] = jnp.concatenate(
            [
                jnp.concatenate(up, axis=1),
                jnp.concatenate([leaf_skel[leaf], leaf_skel[leaf + 1]], axis=1),
                blank,
            ],
            axis=0,
        )
        for each in range(2):
            up_node = up_node + product(up[each], leaf_maps[leaf + each])
    up_sub = product(up_node, node_maps[0])
    packed = jnp.concatenate(
        [
            jnp.concatenate([up_node, up_sub], axis=1),
            jnp.concatenate([node_skel[0], sub_skel[0]], axis=1),
            blank,
        ],
        axis=0,
    )

    def spread(each, carry):
        tree_pack[each] = packed
        return carry

    lax.fori_loop(0, tree_pack.shape[0], spread, 0)
    leave.wait()


def near_kernel(shift, *refs):
    given, (near_out, inverse_out) = refs[:3], refs[3:5]
    held = refs[5:8]
    near, inverse, flat, source, rows, slots = refs[8:14]
    even, odd, sooner, later, sems = refs[14:16], refs[16:18], refs[18:20], refs[20:22], refs[22]
    copies = fetch(list(zip(given, held)), sems)
    crd, perm, tree_vec = held
    count_rows(rows)
    leaves, nvec, block = tree_vec.shape
    chunks = crd.shape[1] // WIDE
    scale, poly = make_tables(1.0 / math.sqrt(block))
    slope = scale[0, 1] - scale[0, 0]
    copies[0].wait()
    for axis in range(2):
        for each in range(chunks):
            row = axis * chunks + each
            flat[row : row + 1, :] = crd[axis : axis + 1, each * WIDE : (each + 1) * WIDE]
    rest = flat[...]
    for piece in range(3):
        rounded = rest.astype(BF16)
        source[piece * 2 * chunks : (piece + 1) * 2 * chunks, :] = rounded
        rest = rest - rounded.astype(F32)
    slots[...] = jnp.zeros_like(slots)
    copies[1].wait()
    side = 128
    tiles = block // side

    def place_leaf(leaf, across, down):
        live = jnp.where(leaf < leaves, 1.0, 0.0)
        leaf = jnp.minimum(leaf, leaves - 1)
        index = leaf_index(perm, leaf, block)
        hot = one_hot(rows, index & (WIDE - 1))
        found = dot(source[...], hot)
        found = (
            found[: 2 * chunks] + found[2 * chunks : 4 * chunks] + found[4 * chunks :]
        )
        mine = lax.broadcasted_iota(jnp.int32, (chunks, block), 0) == index >> SHIFT
        lane = lax.broadcasted_iota(jnp.int32, (chunks, block), 1) + leaf * block
        lane_low = (lane & (WIDE - 1)).astype(F32) * live
        lane_high = (lane >> SHIFT).astype(F32) * live
        marks = jnp.concatenate(
            [jnp.where(mine, lane_low, 0.0), jnp.where(mine, lane_high, 0.0)], axis=0
        ).astype(BF16)
        slots[...] += dot(marks, hot, True)
        row_x = jnp.sum(jnp.where(mine, found[:chunks], 0.0), axis=0, keepdims=True)
        row_y = jnp.sum(jnp.where(mine, found[chunks:], 0.0), axis=0, keepdims=True)
        moved = index + shift[0]
        kind = moved - 3 * ((moved * 43691) >> 17)
        row_w = kind.astype(F32) * slope
        for place, row in enumerate((row_x, row_y, row_w)):
            across[place] = jnp.broadcast_to(row, (8, block))
            turned = jnp.transpose(jnp.broadcast_to(row, (side, block)))
            down[place] = turned.reshape(block // 8, 8, side)

    copies[2].wait()

    def values(across, down, high, low):
        for col in range(tiles):
            cols = slice(col * side, (col + 1) * side)
            over_x, over_y, over_w = [across[each, :, cols] for each in range(3)]
            over_zero, over_one = over_w > 0.5 * slope, over_w > 1.5 * slope

            def across_table(power, first):
                zero, one, two = [float(each) for each in poly[power, first]]
                return jnp.where(over_zero, zero, jnp.where(over_one, one, two))[None]

            table = [[across_table(power, first) for first in range(3)] for power in range(5)]
            over_w = (over_w + float(scale[0, 0]))[None]
            over_x, over_y = over_x[None], over_y[None]
            for row in range(col + 1):
                pieces = []
                for part in range(side // PART):
                    first = row * side + part * PART
                    at = slice(first // 8, (first + PART) // 8)
                    diff_x = down[0, at] - over_x
                    diff_y = down[1, at] - over_y
                    down_w = down[2, at]
                    var_zero, var_one = down_w > 0.5 * slope, down_w > 1.5 * slope
                    square = (diff_x * diff_x + diff_y * diff_y) * (down_w + over_w)
                    arg = square * lax.rsqrt(TINY - square)
                    value = jnp.where(var_one, table[3][1], table[4][2] * arg + table[3][2])
                    rest = value * arg + jnp.where(var_one, table[2][1], table[2][2])
                    value = jnp.where(var_zero, table[2][0], rest)
                    for power in (1, 0):
                        a, b, c = table[power]
                        value = value * arg + jnp.where(var_zero, a, jnp.where(var_one, b, c))
                    pieces.append(parts((value * jnp.exp2(arg)).reshape(PART, side)))
                rows = slice(row * side, (row + 1) * side)
                for each, out in enumerate((high, low)):
                    tile = jnp.concatenate([piece[each] for piece in pieces], axis=0)
                    out[rows, cols] = tile
                    if row < col:
                        out[cols, rows] = jnp.transpose(tile)

    def apply(leaf, high, low):
        vec_hi, vec_lo = parts(tree_vec[leaf])
        both = dot(jnp.concatenate([vec_hi, vec_lo], axis=0), high[...])
        near[leaf] = both[:nvec] + both[nvec:] + dot(vec_hi, low[...])

    for each in later:
        each[...] = jnp.zeros_like(each)

    def two_leaves(step, carry):
        apply(jnp.maximum(2 * step - 1, 0), *later)
        values(*even, *sooner)
        place_leaf(2 * step + 1, *odd)
        apply(2 * step, *sooner)
        values(*odd, *later)
        place_leaf(2 * step + 2, *even)
        return carry

    place_leaf(0, *even)

    lax.fori_loop(0, leaves // 4, two_leaves, 0)
    half = slice(0, leaves // 2 - 1)
    first = pltpu.make_async_copy(near.at[half], near_out.at[half], sems.at[0])
    first.start()
    lax.fori_loop(leaves // 4, leaves // 2, two_leaves, 0)
    inverse[...] = (slots[:chunks] + slots[chunks:] * WIDE).astype(jnp.int32)
    leave = pltpu.make_async_copy(inverse, inverse_out, sems.at[3])
    leave.start()
    apply(leaves - 1, *later)
    half = slice(leaves // 2 - 1, leaves)
    second = pltpu.make_async_copy(near.at[half], near_out.at[half], sems.at[1])
    second.start()
    for copy in (leave, first, second):
        copy.wait()


def far_kernel(groups, subtrees, *refs):
    place, leaf_src, leaf_count, node_src, node_count = refs[:5]
    leaf_packs, refs = refs[5 : 5 + groups], refs[5 + groups :]
    given, out_at, held = refs[:10], refs[10], refs[11:21]
    leaf_all, source, coef, twice, cols, out, rows, srcs, dsts, sems = refs[21:]
    own = leaf_packs[0].shape[0]
    grp_pos = lax.rem(place[0], groups)
    owner = [lax.rem(grp_pos - shift + groups, groups) for shift in range(groups)]
    arrive = [leaf_all.at[pl.ds(each * own, own)] for each in owner]
    copies = fetch(list(zip(leaf_packs + given, arrive + list(held))), sems)
    leaf_copies, copies = copies[:groups], [None] + copies[groups:]
    tree_all, leaf_skel, node_skel, sub_skel, tables = held[:5]
    leaf_maps, node_maps, bases, near, inverse = held[5:]
    count_rows(rows)
    leaves, nvec, block = near.shape
    rank = bases.shape[1]
    nodes = tree_all.shape[0]
    pairs = leaf_all.shape[0]
    node_at = 2 * pairs
    beside = 3 * groups
    sub_at = node_at + beside
    blank = sub_at + subtrees
    sub_pos = lax.div(place[0], groups)
    left = lax.broadcasted_iota(jnp.int32, (PACK_ROWS, 2 * rank), 1) < rank

    def list_leaf(leaf, at):
        count = leaf_count[leaf]

        def one(step, carry):
            srcs[2 * (at + step)] = leaf_src[leaf, 2 * step]
            second = jnp.where(2 * step + 1 < count, leaf_src[leaf, 2 * step + 1], blank)
            srcs[2 * (at + step) + 1] = second
            dsts[at + step] = leaf
            return carry

        steps = (count + 1) // 2
        lax.fori_loop(0, steps, one, 0)
        return at + steps

    size = lax.fori_loop(0, leaves, list_leaf, 0)
    count = node_count[0]

    def list_node(step, carry):
        srcs[2 * (size + step)] = node_at + node_src[0, 2 * step]
        second = jnp.where(2 * step + 1 < count, node_at + node_src[0, 2 * step + 1], blank)
        srcs[2 * (size + step) + 1] = second
        dsts[size + step] = leaves
        return carry

    steps = (count + 1) // 2
    lax.fori_loop(0, steps, list_node, 0)

    def list_sub(sub, at):
        srcs[at] = sub_at + sub
        dsts[at // 2] = leaves + 1
        return at + jnp.where(jnp.abs(sub - sub_pos) >= 2, 1, 0)

    ends = lax.fori_loop(0, subtrees, list_sub, 2 * (size + steps))
    srcs[ends] = blank
    dsts[ends // 2] = leaves + 1
    ends = (ends + 1) // 2
    for each in range(AT_ONCE):
        srcs[2 * (ends + each)] = blank
        srcs[2 * (ends + each) + 1] = blank
        dsts[ends + each] = leaves + 1

    for copy in leaf_copies:
        copy.wait()

    def both_leaves(pair, carry):
        packs = leaf_all[pair]
        turned = pltpu.roll(packs, rank, 1)
        twice[2 * pair] = jnp.where(left, packs, turned)
        twice[2 * pair + 1] = jnp.where(left, turned, packs)
        return carry

    lax.fori_loop(0, pairs, both_leaves, 0, unroll=4)
    copies[1].wait()

    def both_node(each, carry):
        packs = tree_all[jnp.clip((sub_pos - 1) * groups + each, 0, nodes - 1)]
        twice[node_at + each] = jnp.where(left, packs, pltpu.roll(packs, rank, 1))
        return carry

    lax.fori_loop(0, beside, both_node, 0, unroll=4)

    def both_sub(sub, carry):
        total = tree_all[sub * groups, :nvec]
        for each in range(1, groups):
            total = total + tree_all[sub * groups + each, :nvec]
        packs = jnp.concatenate([total, tree_all[sub * groups, nvec:]], axis=0)
        twice[sub_at + sub] = jnp.where(left, pltpu.roll(packs, rank, 1), packs)
        return carry

    lax.fori_loop(0, subtrees, both_sub, 0, unroll=2)
    twice[blank] = jnp.zeros_like(twice[blank])
    coef[...] = jnp.zeros_like(coef)
    for copy in copies[2:6]:
        copy.wait()

    def upright(skel, at):
        for axis in range(2):
            row = jnp.broadcast_to(skel[axis : axis + 1], (2 * rank, rank))
            cols[at, axis] = jnp.transpose(row)

    def upright_leaf(leaf, carry):
        upright(leaf_skel[leaf], leaf)
        return carry

    lax.fori_loop(0, leaves, upright_leaf, 0, unroll=4)
    upright(node_skel[0], leaves)
    upright(sub_skel[0], leaves + 1)

    def couple(step, carry):
        terms = []
        for each in range(AT_ONCE):
            item = step * AT_ONCE + each
            packs = jnp.where(left, twice[srcs[2 * item]], twice[srcs[2 * item + 1]])
            target = dsts[item]
            diff_x = cols[target, 0] - packs[nvec : nvec + 1]
            diff_y = cols[target, 1] - packs[nvec + 1 : nvec + 2]
            square = (diff_x * diff_x + diff_y * diff_y) * tables[0]
            arg = square * lax.rsqrt(TINY - square)
            value = tables[5]
            for power in (4, 3, 2, 1):
                value = value * arg + tables[power]
            value = value * jnp.exp2(arg)
            terms.append((target, product(packs[:nvec], value, True)))
        for target, total in terms:
            coef[target] += total
        return carry

    lax.fori_loop(0, (ends + AT_ONCE - 1) // AT_ONCE, couple, 0)
    for copy in copies[6:]:
        copy.wait()
    down_node = coef[leaves] + product(coef[leaves + 1], node_maps[0], True)
    for leaf in range(leaves):
        down_leaf = coef[leaf] + product(down_node, leaf_maps[leaf], True)
        whole = near[leaf] + product(down_leaf, bases[leaf])
        for each in range(block // WIDE):
            fill(
                source,
                whole[:, each * WIDE : (each + 1) * WIDE],
                (leaf * (block // WIDE) + each) * nvec,
                nvec,
            )

    def scatter(each, carry):
        at = pl.multiple_of(each * block, block)
        out[:, pl.ds(at, block)] = pick(rows, source, leaf_index(inverse, each, block), nvec)
        return carry

    steps = inverse.shape[0] * WIDE // block
    segments = 2
    leaving = []
    for each in range(segments):
        start, stop = each * steps // segments, (each + 1) * steps // segments
        lax.fori_loop(start, stop, scatter, 0, unroll=8)
        span = slice(start * block, stop * block)
        leaving.append(pltpu.make_async_copy(out.at[:, span], out_at.at[:, span], sems.at[each]))
        leaving[-1].start()
    for copy in leaving:
        copy.wait()


def skeleton_tables(rank):
    scale, poly = make_tables(1.0 / math.sqrt(rank))
    var = np.arange(rank) % 3
    rows, cols = var[:, None], np.tile(var, 2)[None, :]
    return np.stack([scale[rows, cols]] + [poly[power][rows, cols] for power in range(5)]).astype(
        np.float32
    )


def shards(
    vectors,
    coords,
    perm,
    bases,
    leaf_maps,
    node_maps,
    leaf_skel,
    node_skel,
    sub_skel,
    leaf_src,
    leaf_count,
    node_src,
    node_count,
):
    nvec, rows_dev = vectors.shape
    leaves, rank, block = bases.shape
    groups = lax.axis_size("grp")
    subtrees = lax.axis_size("leaf")
    nodes = groups * subtrees
    sub_pos = lax.axis_index("leaf")
    device_pos = sub_pos * groups + lax.axis_index("grp")
    chunks = rows_dev // WIDE
    vmem = pl.BlockSpec(memory_space=pltpu.VMEM)
    smem = pl.BlockSpec(memory_space=pltpu.SMEM)
    hbm = pl.BlockSpec(memory_space=pltpu.HBM)
    anywhere = pl.BlockSpec(memory_space=pl.ANY)
    params = pltpu.CompilerParams(vmem_limit_bytes=60 * 1024 * 1024)
    order = perm.reshape(rows_dev // 128, 128)

    def like(*arrays):
        return [pltpu.VMEM(each.shape, each.dtype) for each in arrays]

    given = (vectors, order, bases, leaf_maps, node_maps, leaf_skel, node_skel, sub_skel)
    tree_vec, leaf_pack, tree_pack = pl.pallas_call(
        up_kernel,
        out_shape=(
            jax.ShapeDtypeStruct((leaves, nvec, block), F32),
            jax.ShapeDtypeStruct((leaves // 2, PACK_ROWS, 2 * rank), F32),
            jax.ShapeDtypeStruct((nodes, PACK_ROWS, 2 * rank), F32),
        ),
        in_specs=[hbm] * 8,
        out_specs=(hbm, vmem, vmem),
        scratch_shapes=like(*given)
        + [
            pltpu.VMEM((leaves, nvec, block), F32),
            pltpu.VMEM((chunks * nvec, 2 * WIDE), BF16),
            pltpu.VMEM((WIDE, block), jnp.int16),
            pltpu.SemaphoreType.DMA((9,)),
        ],
        compiler_params=params,
        name="up",
    )(*given)
    tree_all = lax.all_to_all(tree_pack, ("leaf", "grp"), 0, 0, tiled=True)
    leaf_all = [leaf_pack] + [
        lax.ppermute(leaf_pack, "grp", [(each, (each + shift) % groups) for each in range(groups)])
        for shift in range(1, groups)
    ]
    shift = (device_pos * (rows_dev % 3) % 3).astype(jnp.int32).reshape(1)
    near, inverse = pl.pallas_call(
        near_kernel,
        out_shape=(
            jax.ShapeDtypeStruct((leaves, nvec, block), F32),
            jax.ShapeDtypeStruct((chunks, WIDE), jnp.int32),
        ),
        in_specs=[smem, hbm, hbm, hbm],
        out_specs=(hbm,) * 2,
        scratch_shapes=like(coords, order, tree_vec)
        + [
            pltpu.VMEM((leaves, nvec, block), F32),
            pltpu.VMEM((chunks, WIDE), jnp.int32),
            pltpu.VMEM((2 * chunks, WIDE), F32),
            pltpu.VMEM((6 * chunks, WIDE), BF16),
            pltpu.VMEM((WIDE, block), jnp.int16),
            pltpu.VMEM((2 * chunks, WIDE), F32),
            *[
                pltpu.VMEM((3, 8, block), F32),
                pltpu.VMEM((3, block // 8, 8, 128), F32),
            ]
            * 2,
            *[pltpu.VMEM((block, block), BF16)] * 4,
            pltpu.SemaphoreType.DMA((4,)),
        ],
        compiler_params=params,
        cost_estimate=pl.CostEstimate(
            flops=128 * leaves * block * block,
            bytes_accessed=8 * leaves * nvec * block,
            transcendentals=leaves * block * block,
        ),
        name="near",
    )(shift, coords, order, tree_vec)
    tables = jnp.asarray(skeleton_tables(rank))
    given = (tree_all, leaf_skel, node_skel, sub_skel, tables)
    given = given + (leaf_maps, node_maps, bases, near, inverse)
    items = (leaf_src.size + node_src.size + subtrees + 2) // 2 + AT_ONCE
    sources = groups * leaves + 3 * groups + subtrees + 1
    return pl.pallas_call(
        functools.partial(far_kernel, groups, subtrees),
        out_shape=jax.ShapeDtypeStruct((nvec, rows_dev), F32),
        in_specs=[smem] * 5 + [anywhere] * (groups + 1) + [hbm] * 9,
        out_specs=hbm,
        scratch_shapes=like(*given)
        + [
            pltpu.VMEM((groups * leaf_pack.shape[0],) + leaf_pack.shape[1:], F32),
            pltpu.VMEM((chunks * nvec, 2 * WIDE), BF16),
            pltpu.VMEM((leaves + 2, nvec, rank), F32),
            pltpu.VMEM((sources, PACK_ROWS, 2 * rank), F32),
            pltpu.VMEM((leaves + 2, 2, rank, 2 * rank), F32),
            pltpu.VMEM((nvec, rows_dev), F32),
            pltpu.VMEM((WIDE, block), jnp.int16),
            pltpu.SMEM((2 * items,), jnp.int32),
            pltpu.SMEM((items,), jnp.int32),
            pltpu.SemaphoreType.DMA((10 + groups,)),
        ],
        compiler_params=params,
        name="far",
    )(
        device_pos.astype(jnp.int32).reshape(1),
        leaf_src,
        leaf_count,
        node_src,
        node_count,
        *leaf_all,
        *given,
    )


def solution(mesh):
    placed = (
        P(None, ("leaf", "grp")),
        P(None, ("leaf", "grp")),
        P(("leaf", "grp")),
        P(("leaf", "grp"), None, None),
        P(("leaf", "grp"), None, None),
        P(("leaf", "grp"), None, None),
        P(("leaf", "grp"), None, None),
        P(("leaf", "grp"), None, None),
        P("leaf", None, None),
        P(("leaf", "grp"), None),
        P(("leaf", "grp")),
        P(("leaf", "grp"), None),
        P(("leaf", "grp")),
    )
    return jax.shard_map(
        shards, mesh=mesh, in_specs=placed, out_specs=P(None, ("leaf", "grp")), check_vma=False
    )
```

profile of v0, /device:TPU:0, one launch (start us, length us, event | category | flops | bytes accessed | tf_op | source)
XLA Modules:
  0.0 54.9 jit_solution(17177590697319251343)
XLA Ops:
  0.0 8.8 %up.1 = (f32[16,16,512]{2,1,0:T(8,128)}, f32[8,24,128]{2,1,0:T(8,128)}, f32[32,24,128]{2,1,0:T(8,128)}) custom-call(f32[16,8192]{1,0:T(8,128)} %refs_0_.2, s32[64,128]{1,0:T(8,128)} %bitcast.3, f32[16,64,512]{2,1,0:T(8,128)} %refs_16_.1, f32[16,64,64]{2,1,0:T(8,128)} %refs_14_.1, f32[1,64,64]{2,1,0:T(8,128)} %refs_15_.1, f32[16,2,64]{2,1,0:T(2,128)} %refs_10_.1, ...), custom_call_target="tpu_custom_call" | custom-call | tf_op jit(solution)/shard_map/up/pallas_call | solution.py:498
  8.8 7.3 %all-to-all-start = ((f32[32,24,128]{2,1,0:T(8,128)}), f32[32,24,128]{2,1,0:T(8,128)S(1)}, u32[]{:S(2)}, u32[]{:S(2)}) async-start(f32[32,24,128]{2,1,0:T(8,128)} %get-tuple-element.11), calls=%async_computation | async-start | bytes 786432 | tf_op jit(solution)/shard_map/all_to_all | solution.py:517
  16.1 0.3 collective-permute-start
  16.4 1.7 %collective-permute-start.1 = (f32[8,24,128]{2,1,0:T(8,128)}, f32[8,24,128]{2,1,0:T(8,128)S(1)}, u32[]{:S(2)}, u32[]{:S(2)}) collective-permute-start(f32[8,24,128]{2,1,0:T(8,128)} %get-tuple-element.10.refs_5_), channel_id=1, source_target_pairs={{0,2},{1,3},{2,0},{3,1},{4,6},{5,7},{6,4},{7,5},{8,10},{9,11},{10,... | collective-permute-start | bytes 294920 | tf_op jit(solution)/shard_map/ppermute | solution.py:519
  18.1 1.3 %collective-permute-start.2 = (f32[8,24,128]{2,1,0:T(8,128)}, f32[8,24,128]{2,1,0:T(8,128)S(1)}, u32[]{:S(2)}, u32[]{:S(2)}) collective-permute-start(f32[8,24,128]{2,1,0:T(8,128)} %get-tuple-element.10.refs_5_), channel_id=1, source_target_pairs={{0,3},{1,0},{2,1},{3,2},{4,7},{5,4},{6,5},{7,6},{8,11},{9,8},{10,9... | collective-permute-start | bytes 294920 | tf_op jit(solution)/shard_map/ppermute | solution.py:519
  20.1 20.1 %near.1 = (f32[16,16,512]{2,1,0:T(8,128)}, s32[64,128]{1,0:T(8,128)}) custom-call(s32[1]{0:T(128)} %bitcast.2.shift, f32[2,8192]{1,0:T(2,128)} %refs_0_.3, s32[64,128]{1,0:T(8,128)} %bitcast.4, f32[16,16,512]{2,1,0:T(8,128)} %get-tuple-element.12.refs_2_), custom_call_target="tpu_custom_call" | custom-call | flops 536870912 | bytes 1048576 | tf_op jit(solution)/shard_map/near/pallas_call | solution.py:523
  40.2 0.0 collective-permute-done.refs_6_
  40.2 0.0 copy-start.1
  40.2 0.0 collective-permute-done.1.refs_7_
  40.2 0.0 copy-start.2
  40.2 0.0 collective-permute-done.2.refs_8_
  40.2 0.0 copy-start.3
  40.2 0.0 all-to-all-done.refs_9_
  40.2 0.0 copy-start
  40.3 0.6 %copy-done.1 = f32[8,24,128]{2,1,0:T(8,128)} copy-done((f32[8,24,128]{2,1,0:T(8,128)}, f32[8,24,128]{2,1,0:T(8,128)S(1)}, u32[]{:S(2)}) %copy-start.1) | copy-done | bytes 98328
  40.8 0.0 copy-done.2
  40.9 0.0 copy-done.3
  40.9 0.2 copy-done
  41.1 13.7 %far.1 = f32[16,8192]{1,0:T(8,128)} custom-call(s32[1]{0:T(128)} %bitcast.refs_0_, s32[16,16]{1,0:T(8,128)} %refs_1_.1, s32[16]{0:T(128)} %refs_2_.3, s32[1,8]{1,0:T(1,128)} %refs_3_.3, s32[1]{0:T(128)S(6)} %copy.15.refs_4_, f32[8,24,128]{2,1,0:T(8,128)} %get-tuple-element.10.refs_5_, f32[8,24,128]{2,1,0:T(8,128)} %copy-done.1, f32[8,24,128]{2,1,0:T(8,128)} %copy-done.2, ...), custom_call_target="tpu_custom_call" | custom-call | tf_op jit(solution)/shard_map/far/pallas_call | solution.py:560
Async XLA Ops:
  8.8 31.4 %all-to-all-start = ((f32[32,24,128]{2,1,0:T(8,128)}), f32[32,24,128]{2,1,0:T(8,128)S(1)}, u32[]{:S(2)}, u32[]{:S(2)}) async-start(f32[32,24,128]{2,1,0:T(8,128)} %get-tuple-element.11), calls=%async_computation | async-start | bytes 786432 | tf_op jit(solution)/shard_map/all_to_all | solution.py:517
  16.1 24.0 %collective-permute-start = (f32[8,24,128]{2,1,0:T(8,128)}, f32[8,24,128]{2,1,0:T(8,128)S(1)}, u32[]{:S(2)}, u32[]{:S(2)}) collective-permute-start(f32[8,24,128]{2,1,0:T(8,128)} %get-tuple-element.10.refs_5_), channel_id=1, source_target_pairs={{0,1},{1,2},{2,3},{3,0},{4,5},{5,6},{6,7},{7,4},{8,9},{9,10},{10,1... | collective-permute-start | bytes 294920 | tf_op jit(solution)/shard_map/ppermute | solution.py:519
  16.4 23.8 %collective-permute-start.1 = (f32[8,24,128]{2,1,0:T(8,128)}, f32[8,24,128]{2,1,0:T(8,128)S(1)}, u32[]{:S(2)}, u32[]{:S(2)}) collective-permute-start(f32[8,24,128]{2,1,0:T(8,128)} %get-tuple-element.10.refs_5_), channel_id=1, source_target_pairs={{0,2},{1,3},{2,0},{3,1},{4,6},{5,7},{6,4},{7,5},{8,10},{9,11},{10,... | collective-permute-start | bytes 294920 | tf_op jit(solution)/shard_map/ppermute | solution.py:519
  18.1 22.1 %collective-permute-start.2 = (f32[8,24,128]{2,1,0:T(8,128)}, f32[8,24,128]{2,1,0:T(8,128)S(1)}, u32[]{:S(2)}, u32[]{:S(2)}) collective-permute-start(f32[8,24,128]{2,1,0:T(8,128)} %get-tuple-element.10.refs_5_), channel_id=1, source_target_pairs={{0,3},{1,0},{2,1},{3,2},{4,7},{5,4},{6,5},{7,6},{8,11},{9,8},{10,9... | collective-permute-start | bytes 294920 | tf_op jit(solution)/shard_map/ppermute | solution.py:519
  40.2 0.6 %copy-start.1 = (f32[8,24,128]{2,1,0:T(8,128)}, f32[8,24,128]{2,1,0:T(8,128)S(1)}, u32[]{:S(2)}) copy-start(f32[8,24,128]{2,1,0:T(8,128)S(1)} %collective-permute-done.refs_6_) | copy-start | bytes 294916
  40.2 0.7 %copy-start.2 = (f32[8,24,128]{2,1,0:T(8,128)}, f32[8,24,128]{2,1,0:T(8,128)S(1)}, u32[]{:S(2)}) copy-start(f32[8,24,128]{2,1,0:T(8,128)S(1)} %collective-permute-done.1.refs_7_) | copy-start | bytes 294916
  40.2 0.7 %copy-start.3 = (f32[8,24,128]{2,1,0:T(8,128)}, f32[8,24,128]{2,1,0:T(8,128)S(1)}, u32[]{:S(2)}) copy-start(f32[8,24,128]{2,1,0:T(8,128)S(1)} %collective-permute-done.2.refs_8_) | copy-start | bytes 294916
  40.2 0.8 %copy-start = (f32[32,24,128]{2,1,0:T(8,128)}, f32[32,24,128]{2,1,0:T(8,128)S(1)}, u32[]{:S(2)}) copy-start(f32[32,24,128]{2,1,0:T(8,128)S(1)} %all-to-all-done.refs_9_) | copy-start | bytes 1179652
where the time goes:
time: 55.9 us; the launch traced here: 54.9 us
  Pallas kernels  42.6 us (76%)
  starting transfers between devices  10.6 us (19%)
  between operations  0.91 us (2%)
  local copies, waits for them, and re-layouts  0.82 us (1%)
    pallas_call x1, Pallas kernels, shards(): pl.pallas_call(near_kernel, out_shape=(jax.ShapeDtypeStruct((leaves, nvec...  20.1 us
    pallas_call x1, Pallas kernels, shards(): pl.pallas_call(functools.partial(far_kernel, groups, subtrees), out_shape...  13.7 us
    pallas_call x1, Pallas kernels, shards(): pl.pallas_call(up_kernel, out_shape=(jax.ShapeDtypeStruct((leaves, nvec,...  8.81 us
    all_to_all x1, starting transfers between devices, shards(): tree_all = lax.all_to_all(tree_pack, ('leaf', 'grp'), 0, 0, tiled=True)  7.3 us
    ppermute x3, starting transfers between devices, shards(): lax.ppermute(leaf_pack, 'grp', [(each, (each + shift) % groups) for each...  3.3 us
  transfers between devices with their start and end apart: 4, of which 0 were waited for; matrix products, arithmetic and copies ran while one was open for 0% of the time, Pallas kernels for 37%

commit v1 on v0

--- a/solution.py
+++ b/solution.py
@@ -17,7 +17,7 @@
 TINY = 1e-37
 PACK_ROWS = 24
 PART = 32
-AT_ONCE = 8
+AT_ONCE = 16
 
 
 def make_tables(norm):
@@ -121,7 +121,7 @@
         tree_vec[leaf] = pick(rows, source, leaf_index(perm, leaf, block), nvec)
         return carry
 
-    lax.fori_loop(0, leaves, gather, 0, unroll=8)
+    lax.fori_loop(0, leaves, gather, 0, unroll=16)
     leave = pltpu.make_async_copy(tree_vec, tree_out, sems.at[len(copies)])
     leave.start()
     for copy in copies[2:]:

time: 55.9 us -> 56.1 us (level); the launches traced: 54.9 us -> 56.5 us
  Pallas kernels: 42.6 us -> 44.2 us
    pallas_call x1, Pallas kernels: 13.7 us -> 15.5 us  [shards(): pl.pallas_call(functools.partial(far_kernel, groups, subtrees), out_shape...]
  transfers between devices with their start and end apart: 4 -> 4, of which waited for: 0 -> 0; matrix products, arithmetic and copies ran while one was open for 0% -> 0% of each run, Pallas kernels for 37% -> 36%
where the time goes in v1:
time: 56.1 us; the launch traced here: 56.5 us
  Pallas kernels  44.2 us (79%)
  starting transfers between devices  10.6 us (19%)
  between operations  0.91 us (2%)
  local copies, waits for them, and re-layouts  0.82 us (1%)
    pallas_call x1, Pallas kernels, shards(): pl.pallas_call(near_kernel, out_shape=(jax.ShapeDtypeStruct((leaves, nvec...  20.1 us
    pallas_call x1, Pallas kernels, shards(): pl.pallas_call(functools.partial(far_kernel, groups, subtrees), out_shape...  15.5 us
    pallas_call x1, Pallas kernels, shards(): pl.pallas_call(up_kernel, out_shape=(jax.ShapeDtypeStruct((leaves, nvec,...  8.62 us
    all_to_all x1, starting transfers between devices, shards(): tree_all = lax.all_to_all(tree_pack, ('leaf', 'grp'), 0, 0, tiled=True)  7.3 us
    ppermute x3, starting transfers between devices, shards(): lax.ppermute(leaf_pack, 'grp', [(each, (each + shift) % groups) for each...  3.3 us
  transfers between devices with their start and end apart: 4, of which 0 were waited for; matrix products, arithmetic and copies ran while one was open for 0% of the time, Pallas kernels for 36%

profile of v1, /device:TPU:0, one launch (start us, length us, event | category | flops | bytes accessed | tf_op | source)
XLA Modules:
  0.0 56.5 jit_solution(11544106327201171273)
XLA Ops:
  0.0 8.6 %up.1 = (f32[16,16,512]{2,1,0:T(8,128)}, f32[8,24,128]{2,1,0:T(8,128)}, f32[32,24,128]{2,1,0:T(8,128)}) custom-call(f32[16,8192]{1,0:T(8,128)} %refs_0_.2, s32[64,128]{1,0:T(8,128)} %bitcast.3, f32[16,64,512]{2,1,0:T(8,128)} %refs_16_.1, f32[16,64,64]{2,1,0:T(8,128)} %refs_14_.1, f32[1,64,64]{2,1,0:T(8,128)} %refs_15_.1, f32[16,2,64]{2,1,0:T(2,128)} %refs_10_.1, ...), custom_call_target="tpu_custom_call" | custom-call | tf_op jit(solution)/shard_map/up/pallas_call | solution.py:498
  8.6 7.3 %all-to-all-start = ((f32[32,24,128]{2,1,0:T(8,128)}), f32[32,24,128]{2,1,0:T(8,128)S(1)}, u32[]{:S(2)}, u32[]{:S(2)}) async-start(f32[32,24,128]{2,1,0:T(8,128)} %get-tuple-element.11), calls=%async_computation | async-start | bytes 786432 | tf_op jit(solution)/shard_map/all_to_all | solution.py:517
  15.9 0.3 collective-permute-start
  16.2 1.7 %collective-permute-start.1 = (f32[8,24,128]{2,1,0:T(8,128)}, f32[8,24,128]{2,1,0:T(8,128)S(1)}, u32[]{:S(2)}, u32[]{:S(2)}) collective-permute-start(f32[8,24,128]{2,1,0:T(8,128)} %get-tuple-element.10.refs_5_), channel_id=1, source_target_pairs={{0,2},{1,3},{2,0},{3,1},{4,6},{5,7},{6,4},{7,5},{8,10},{9,11},{10,... | collective-permute-start | bytes 294920 | tf_op jit(solution)/shard_map/ppermute | solution.py:519
  17.9 1.3 %collective-permute-start.2 = (f32[8,24,128]{2,1,0:T(8,128)}, f32[8,24,128]{2,1,0:T(8,128)S(1)}, u32[]{:S(2)}, u32[]{:S(2)}) collective-permute-start(f32[8,24,128]{2,1,0:T(8,128)} %get-tuple-element.10.refs_5_), channel_id=1, source_target_pairs={{0,3},{1,0},{2,1},{3,2},{4,7},{5,4},{6,5},{7,6},{8,11},{9,8},{10,9... | collective-permute-start | bytes 294920 | tf_op jit(solution)/shard_map/ppermute | solution.py:519
  19.9 20.1 %near.1 = (f32[16,16,512]{2,1,0:T(8,128)}, s32[64,128]{1,0:T(8,128)}) custom-call(s32[1]{0:T(128)} %bitcast.2.shift, f32[2,8192]{1,0:T(2,128)} %refs_0_.3, s32[64,128]{1,0:T(8,128)} %bitcast.4, f32[16,16,512]{2,1,0:T(8,128)} %get-tuple-element.12.refs_2_), custom_call_target="tpu_custom_call" | custom-call | flops 536870912 | bytes 1048576 | tf_op jit(solution)/shard_map/near/pallas_call | solution.py:523
  40.0 0.0 collective-permute-done.refs_6_
  40.0 0.0 copy-start.1
  40.0 0.0 collective-permute-done.1.refs_7_
  40.0 0.0 copy-start.2
  40.0 0.0 collective-permute-done.2.refs_8_
  40.0 0.0 copy-start.3
  40.0 0.0 all-to-all-done.refs_9_
  40.1 0.0 copy-start
  40.1 0.6 %copy-done.1 = f32[8,24,128]{2,1,0:T(8,128)} copy-done((f32[8,24,128]{2,1,0:T(8,128)}, f32[8,24,128]{2,1,0:T(8,128)S(1)}, u32[]{:S(2)}) %copy-start.1) | copy-done | bytes 98328
  40.6 0.0 copy-done.2
  40.7 0.0 copy-done.3
  40.7 0.2 copy-done
  40.9 15.5 %far.1 = f32[16,8192]{1,0:T(8,128)} custom-call(s32[1]{0:T(128)} %bitcast.refs_0_, s32[16,16]{1,0:T(8,128)} %refs_1_.1, s32[16]{0:T(128)} %refs_2_.3, s32[1,8]{1,0:T(1,128)} %refs_3_.3, s32[1]{0:T(128)S(6)} %copy.15.refs_4_, f32[8,24,128]{2,1,0:T(8,128)} %get-tuple-element.10.refs_5_, f32[8,24,128]{2,1,0:T(8,128)} %copy-done.1, f32[8,24,128]{2,1,0:T(8,128)} %copy-done.2, ...), custom_call_target="tpu_custom_call" | custom-call | tf_op jit(solution)/shard_map/far/pallas_call | solution.py:560
Async XLA Ops:
  8.6 31.4 %all-to-all-start = ((f32[32,24,128]{2,1,0:T(8,128)}), f32[32,24,128]{2,1,0:T(8,128)S(1)}, u32[]{:S(2)}, u32[]{:S(2)}) async-start(f32[32,24,128]{2,1,0:T(8,128)} %get-tuple-element.11), calls=%async_computation | async-start | bytes 786432 | tf_op jit(solution)/shard_map/all_to_all | solution.py:517
  15.9 24.0 %collective-permute-start = (f32[8,24,128]{2,1,0:T(8,128)}, f32[8,24,128]{2,1,0:T(8,128)S(1)}, u32[]{:S(2)}, u32[]{:S(2)}) collective-permute-start(f32[8,24,128]{2,1,0:T(8,128)} %get-tuple-element.10.refs_5_), channel_id=1, source_target_pairs={{0,1},{1,2},{2,3},{3,0},{4,5},{5,6},{6,7},{7,4},{8,9},{9,10},{10,1... | collective-permute-start | bytes 294920 | tf_op jit(solution)/shard_map/ppermute | solution.py:519
  16.2 23.8 %collective-permute-start.1 = (f32[8,24,128]{2,1,0:T(8,128)}, f32[8,24,128]{2,1,0:T(8,128)S(1)}, u32[]{:S(2)}, u32[]{:S(2)}) collective-permute-start(f32[8,24,128]{2,1,0:T(8,128)} %get-tuple-element.10.refs_5_), channel_id=1, source_target_pairs={{0,2},{1,3},{2,0},{3,1},{4,6},{5,7},{6,4},{7,5},{8,10},{9,11},{10,... | collective-permute-start | bytes 294920 | tf_op jit(solution)/shard_map/ppermute | solution.py:519
  17.9 22.1 %collective-permute-start.2 = (f32[8,24,128]{2,1,0:T(8,128)}, f32[8,24,128]{2,1,0:T(8,128)S(1)}, u32[]{:S(2)}, u32[]{:S(2)}) collective-permute-start(f32[8,24,128]{2,1,0:T(8,128)} %get-tuple-element.10.refs_5_), channel_id=1, source_target_pairs={{0,3},{1,0},{2,1},{3,2},{4,7},{5,4},{6,5},{7,6},{8,11},{9,8},{10,9... | collective-permute-start | bytes 294920 | tf_op jit(solution)/shard_map/ppermute | solution.py:519
  40.0 0.6 %copy-start.1 = (f32[8,24,128]{2,1,0:T(8,128)}, f32[8,24,128]{2,1,0:T(8,128)S(1)}, u32[]{:S(2)}) copy-start(f32[8,24,128]{2,1,0:T(8,128)S(1)} %collective-permute-done.refs_6_) | copy-start | bytes 294916
  40.0 0.7 %copy-start.2 = (f32[8,24,128]{2,1,0:T(8,128)}, f32[8,24,128]{2,1,0:T(8,128)S(1)}, u32[]{:S(2)}) copy-start(f32[8,24,128]{2,1,0:T(8,128)S(1)} %collective-permute-done.1.refs_7_) | copy-start | bytes 294916
  40.0 0.7 %copy-start.3 = (f32[8,24,128]{2,1,0:T(8,128)}, f32[8,24,128]{2,1,0:T(8,128)S(1)}, u32[]{:S(2)}) copy-start(f32[8,24,128]{2,1,0:T(8,128)S(1)} %collective-permute-done.2.refs_8_) | copy-start | bytes 294916
  40.1 0.8 %copy-start = (f32[32,24,128]{2,1,0:T(8,128)}, f32[32,24,128]{2,1,0:T(8,128)S(1)}, u32[]{:S(2)}) copy-start(f32[32,24,128]{2,1,0:T(8,128)S(1)} %all-to-all-done.refs_9_) | copy-start | bytes 1179652
